TPU v7x, 512 devices: a whole 4x8x8 slice. The times are simulated.
512 devices in a mesh: gx: 8 (over y_hi, core), gy: 8 (over z), gz: 8 (over x, y_lo).
Axes of the slice: x: 4, y: 8 (y_hi: 4, y_lo: 2; y = y_hi * 2 + y_lo), z: 8, core: 2. Of those that a mesh axis runs over, the one named last changes fastest.
Arguments:
- orbital_values: bfloat16 [128, 128, 192, 384], P('gx', 'gy', 'gz'), may hold values from -6 to 6
- dm_slabs: bfloat16 [24576, 8, 384], P(('gx', 'gy', 'gz')), may hold values from -0.015625 to 0.015625
- slab_tile: int32 [24576], P(('gx', 'gy', 'gz')), may hold values from 0 to 63, as said below
- slab_place: int32 [24576], P(('gx', 'gy', 'gz')), may hold values from 0 to 47, as said below
Outputs:
- potential: float32 [128, 128, 192], P('gx', 'gy', 'gz')
- pot_slabs: bfloat16 [24576, 8, 384], P(('gx', 'gy', 'gz'))
Inputs may be any that keep to these rules, and one draw needn't show every extreme that they name: `slab_tile`: within each layer along gz, every tile of that layer has exactly one slab for each place 0 .. 47, held by devices of the same layer; no device holds more than 2 slabs of one tile, and in every layer some device holds exactly 2 slabs of some tile. See slab_tile: the pair (slab_tile, slab_place) is different for all slabs of one layer.
All inputs are finite; a program needn't handle non-finite values.
Results may differ from a plain program's by a relative error of at most 0.0023.
Values may be sent and summed in bfloat16 or wider, within the bound.
A program may use at most 64 MiB of HBM per device.

v0:
```python
import math

import jax
import jax.numpy as jnp
from jax import lax
from jax.sharding import PartitionSpec as P

RADIUS = 8


ALPHAS = (0.012, 0.025, 0.05, 0.1, 0.2, 0.4, 0.8, 1.6)
MIXES = (0.3, 0.3, 0.32, 0.34, 0.36, 0.38, 0.4, 0.42)


def with_halo(shard, sides, width):
    for axis, dim in sides:
        size, length = (lax.axis_size(axis), shard.shape[dim])
        up = [(i, (i + 1) % size) for i in range(size)]
        down = [(j, i) for i, j in up]
        last = lax.slice_in_dim(shard, length - width, length, axis=dim)
        initial = lax.slice_in_dim(shard, 0, width, axis=dim)
        before = lax.ppermute(last, axis, up)
        after = lax.ppermute(initial, axis, down)
        shard = jnp.concatenate([before, shard, after], axis=dim)
    return shard


def kernel_tables(radius):
    tap_table = [
        [math.exp(-alpha * offset * offset) for offset in range(-radius, radius + 1)]
        for alpha in ALPHAS
    ]
    mix = [
        MIXES[term] / sum((tap * tap for tap in tap_table[term])) ** 1.5
        for term in range(len(ALPHAS))
    ]
    return (tap_table, mix)


def smooth_along(stacked, axis_idx, count, tap_table):
    running = None
    for offset in range(len(tap_table[0])):
        tap_column = jnp.asarray([row[offset] for row in tap_table], dtype=jnp.float32).reshape(
            -1, 1, 1, 1
        )
        addend = tap_column * lax.slice_in_dim(stacked, offset, offset + count, axis=axis_idx)
        running = addend if running is None else running + addend
    return running


def combine_terms(stacked, mix):
    potential = None
    for term_idx in range(stacked.shape[0]):
        addend = mix[term_idx] * stacked[term_idx]
        potential = addend if potential is None else potential + addend
    return potential


def rank_within(key_ids, bucket_ids, is_valid):
    same_bucket = (bucket_ids[:, None] == bucket_ids[None, :]) & is_valid[None, :]
    earlier = key_ids[None, :] < key_ids[:, None]
    return jnp.sum(same_bucket & earlier, axis=1)


def pack_slots(slot_ids, payload, key_ids, slot_count):
    one_hot = slot_ids[:, None] == jnp.arange(slot_count, dtype=jnp.int32)[None, :]
    hot_matrix = one_hot.astype(jnp.bfloat16)
    shipped = jnp.dot(hot_matrix.T, payload, preferred_element_type=jnp.float32).astype(
        jnp.bfloat16
    )
    labels = jnp.sum(jnp.where(one_hot, key_ids[:, None] + 1, 0), axis=0) - 1
    return (hot_matrix, shipped, labels)


def unpack_slots(hot_matrix, arrived):
    return jnp.dot(hot_matrix, arrived, preferred_element_type=jnp.float32).astype(jnp.bfloat16)


def local(orbital_values, dm_slabs, slab_tile, slab_place):
    size_x, size_y, size_z, list_orb = orbital_values.shape
    slab_count, atom_orb, _ = dm_slabs.shape
    list_blk = list_orb // atom_orb
    row_width = atom_orb * list_orb
    across_x = lax.axis_size("gx")
    across_y = lax.axis_size("gy")
    tile_count = across_x * across_y
    capacity = max(2, 2 * ((list_blk + tile_count - 1) // tile_count))
    payload = dm_slabs.reshape(slab_count, row_width)
    key_ids = slab_tile * list_blk + slab_place
    all_valid = jnp.ones((slab_count,), dtype=bool)
    tile_points = size_x * size_y * size_z
    values = orbital_values.reshape(tile_points, list_orb)
    direct_slots = slab_tile * capacity + rank_within(key_ids, slab_tile, all_valid)
    direct_hot, direct_out, direct_keys = pack_slots(
        direct_slots, payload, key_ids, tile_count * capacity
    )
    arrived, arrived_keys = (
        lax.all_to_all(
            direct_out.reshape(tile_count, capacity, row_width),
            ("gx", "gy"),
            split_axis=0,
            concat_axis=0,
            tiled=True,
        ),
        lax.all_to_all(
            direct_keys.reshape(tile_count, capacity),
            ("gx", "gy"),
            split_axis=0,
            concat_axis=0,
            tiled=True,
        ),
    )
    arrived_keys = arrived_keys.reshape(-1)
    places = jnp.where(arrived_keys >= 0, arrived_keys % list_blk, -1)
    place_hot = (places[:, None] == jnp.arange(list_blk, dtype=jnp.int32)[None, :]).astype(
        jnp.bfloat16
    )
    tile_matrix = (
        jnp.dot(place_hot.T, arrived.reshape(-1, row_width), preferred_element_type=jnp.float32)
        .astype(jnp.bfloat16)
        .reshape(list_orb, list_orb)
    )
    product = jnp.dot(values, tile_matrix, preferred_element_type=jnp.float32)
    density = jnp.sum(product * values.astype(jnp.float32), axis=1).reshape(size_x, size_y, size_z)
    tap_table, mix = kernel_tables(RADIUS)
    padded = with_halo(density, (("gx", 0),), RADIUS)[None]
    stacked = smooth_along(padded, 1, size_x, tap_table)
    stacked = smooth_along(with_halo(stacked, (("gy", 2),), RADIUS), 2, size_y, tap_table)
    stacked = smooth_along(with_halo(stacked, (("gz", 3),), RADIUS), 3, size_z, tap_table)
    potential = combine_terms(stacked, mix)
    quad_weight = float(tile_points) ** (-0.5)
    weighted = (
        potential.reshape(tile_points, 1) * values.astype(jnp.float32) * quad_weight
    ).astype(jnp.bfloat16)
    tile_potential = lax.dot_general(
        values, weighted, (((0,), (0,)), ((), ())), preferred_element_type=jnp.float32
    ).astype(jnp.bfloat16)
    pot_rows = tile_potential.reshape(list_blk, row_width)
    returned = jnp.dot(place_hot, pot_rows, preferred_element_type=jnp.float32).astype(jnp.bfloat16)
    back_home = lax.all_to_all(
        returned.reshape(tile_count, capacity, row_width),
        ("gx", "gy"),
        split_axis=0,
        concat_axis=0,
        tiled=True,
    )
    own_rows = unpack_slots(direct_hot, back_home.reshape(-1, row_width))
    return (potential, own_rows.reshape(slab_count, atom_orb, list_orb))


def solution(mesh):
    placed = (
        P("gx", "gy", "gz", None),
        P(("gx", "gy", "gz"), None, None),
        P(("gx", "gy", "gz")),
        P(("gx", "gy", "gz")),
    )
    return jax.shard_map(
        local,
        mesh=mesh,
        in_specs=placed,
        out_specs=(P("gx", "gy", "gz"), P(("gx", "gy", "gz"), None, None)),
        check_vma=False,
    )
```

profile of v0, /device:TPU:1, one launch (start us, length us, event | category | flops | bytes accessed | tf_op | source)
XLA Modules:
  0.0 187.0 jit_solution(15530218885836999719)
XLA Ops:
  0.6 0.7 broadcast_add_fusion.1
  1.3 0.9 convert_reduce_fusion
  2.2 0.7 multiply_add_fusion.2
  3.0 0.8 sub.7
  3.8 17.6 %all-to-all-start = ((s32[64,1,2]{2,1,0:T(1,128)}), s32[64,1,2]{2,1,0:T(1,128)S(1)}, u32[]{:S(2)}, u32[]{:S(2)}) async-start(s32[64,1,2]{2,1,0:T(1,128)} %bitcast), calls=%async_computation | async-start | bytes 65536 | tf_op jit(solution)/shard_map/all_to_all | solution.py:105
  21.4 1.0 copy.102
  22.4 0.5 convolution_convert_fusion.1
  22.9 1.2 reshape.272
  24.1 8.8 %all-to-all-done = s32[64,1,2]{2,1,0:T(1,128)S(1)} async-done(((s32[64,1,2]{2,1,0:T(1,128)}), s32[64,1,2]{2,1,0:T(1,128)S(1)}, u32[]{:S(2)}, u32[]{:S(2)}) %all-to-all-start) | async-done | bytes 544 | tf_op jit(solution)/shard_map/all_to_all | solution.py:105
  32.9 5.0 %all-to-all-start.1 = ((bf16[64,2,3072]{2,1,0:T(2,128)(2,1)}), bf16[64,2,3072]{2,1,0:T(2,128)(2,1)S(1)}, u32[]{:S(2)}, u32[]{:S(2)}) async-start(bf16[64,2,3072]{2,1,0:T(2,128)(2,1)} %reshape.272), calls=%async_computation.1 | async-start | bytes 1572864 | tf_op jit(solution)/shard_map/all_to_all | solution.py:98
  37.9 6.7 %copy.95 = bf16[6144,384]{0,1:T(8,128)(2,1)} copy(bf16[6144,384]{1,0:T(8,128)(2,1)} %bitcast.65) | data formatting | bytes 9437184 | tf_op jit(solution)/shard_map/reshape | solution.py:92
  45.1 18.8 %all-to-all-done.1 = bf16[64,2,3072]{2,1,0:T(2,128)(2,1)S(1)} async-done(((bf16[64,2,3072]{2,1,0:T(2,128)(2,1)}), bf16[64,2,3072]{2,1,0:T(2,128)(2,1)S(1)}, u32[]{:S(2)}, u32[]{:S(2)}) %all-to-all-start.1) | async-done | bytes 786464 | tf_op jit(solution)/shard_map/all_to_all | solution.py:98
  64.8 6.4 %fusion = f32[6144]{0:T(1024)S(1)} fusion(bf16[6144,384]{0,1:T(8,128)(2,1)} %copy.95, bf16[384,384]{1,0:T(8,128)(2,1)S(1)} %reshape.274, bf16[6144,384]{1,0:T(8,128)(2,1)} %bitcast.66), kind=kOutput, calls=%fused_computation.1 | convolution fusion | flops 1819011072 | bytes 9756672 | tf_op jit(solution)/shard_map/dot_general | solution.py:123
  71.5 2.8 %collective-permute-start.1 = (f32[8,16,24]{2,1,0:T(8,128)S(1)}, f32[8,16,24]{2,1,0:T(8,128)S(1)}, u32[]{:S(2)}, u32[]{:S(2)}) collective-permute-start(f32[8,16,24]{2,1,0:T(8,128)S(1)} %slice.246), channel_id=1, source_target_pairs={{64,0},{128,64},{192,128},{256,192},{320,256},{384,320},{448,384},... | collective-permute-start | bytes 36872 | tf_op jit(solution)/shard_map/ppermute | solution.py:23
  74.3 4.5 %collective-permute-start = (f32[8,16,24]{2,1,0:T(8,128)S(1)}, f32[8,16,24]{2,1,0:T(8,128)S(1)}, u32[]{:S(2)}, u32[]{:S(2)}) collective-permute-start(f32[8,16,24]{2,1,0:T(8,128)S(1)} %slice.244), channel_id=1, source_target_pairs={{0,64},{64,128},{128,192},{192,256},{256,320},{320,384},{384,448},... | collective-permute-start | bytes 36872 | tf_op jit(solution)/shard_map/ppermute | solution.py:22
  79.0 1.2 collective-permute-done
  80.4 1.3 multiply_add_fusion
  81.9 1.9 %collective-permute-start.2 = (f32[8,16,8,24]{3,2,1,0:T(8,128)S(1)}, f32[8,16,8,24]{3,2,1,0:T(8,128)S(1)}, u32[]{:S(2)}, u32[]{:S(2)}) collective-permute-start(f32[8,16,8,24]{3,2,1,0:T(8,128)S(1)} %get-tuple-element.10), channel_id=1, source_target_pairs={{0,8},{8,16},{16,24},{24,32},{32,40},{40,48},{48,56},{56,0},{1,9},... | collective-permute-start | bytes 294920 | tf_op jit(solution)/shard_map/ppermute | solution.py:22
  83.8 4.6 %collective-permute-start.3 = (f32[8,16,8,24]{3,2,1,0:T(8,128)S(1)}, f32[8,16,8,24]{3,2,1,0:T(8,128)S(1)}, u32[]{:S(2)}, u32[]{:S(2)}) collective-permute-start(f32[8,16,8,24]{3,2,1,0:T(8,128)S(1)} %get-tuple-element.11), channel_id=1, source_target_pairs={{8,0},{16,8},{24,16},{32,24},{40,32},{48,40},{56,48},{0,56},{9,1},... | collective-permute-start | bytes 294920 | tf_op jit(solution)/shard_map/ppermute | solution.py:23
  88.4 6.8 %collective-permute-done.2 = f32[8,16,8,24]{3,2,1,0:T(8,128)S(1)} collective-permute-done((f32[8,16,8,24]{3,2,1,0:T(8,128)S(1)}, f32[8,16,8,24]{3,2,1,0:T(8,128)S(1)}, u32[]{:S(2)}, u32[]{:S(2)}) %collective-permute-start.2) | collective-permute-done | bytes 98336 | tf_op jit(solution)/shard_map/ppermute | solution.py:22
  95.1 0.9 collective-permute-done.3
  96.0 3.1 %fusion.10 = f32[8,16,16,24]{3,2,1,0:T(8,128)S(1)} fusion(f32[8,16,16,24]{3,2,1,0:T(8,128)S(1)} %multiply_add_fusion, f32[8,16,8,24]{3,2,1,0:T(8,128)S(1)} %collective-permute-done.3, f32[8,16,8,24]{3,2,1,0:T(8,128)S(1)} %collective-permute-done.2, f32[8]{0:T(128)S(1)} %copy-done.1, f32[8]{0:T(128)S(1)} %copy-done.2, f32[8]{0:T(128)S(1)} %copy-done.3, ...), kind=kLoop, calls=%fused_computation.44 | loop fusion | flops 2359296 | bytes 590080 | tf_op jit(solution)/shard_map/add | solution.py:47
  99.5 1.1 copy.98
  100.6 1.9 %collective-permute-start.5 = (f32[8,16,16,8]{2,3,1,0:T(8,128)}, f32[8,16,16,8]{2,3,1,0:T(8,128)S(1)}, u32[]{:S(2)}, u32[]{:S(2)}) collective-permute-start(f32[8,16,16,8]{2,3,1,0:T(8,128)} %copy.98), channel_id=1, source_target_pairs={{1,0},{2,1},{3,2},{4,3},{5,4},{6,5},{7,6},{0,7},{9,8},{10,9},{11,1... | collective-permute-start | bytes 196616 | tf_op jit(solution)/shard_map/ppermute | solution.py:23
  102.9 3.6 %collective-permute-start.4 = (f32[8,16,16,8]{2,3,1,0:T(8,128)S(1)}, f32[8,16,16,8]{2,3,1,0:T(8,128)}, u32[]{:S(2)}, u32[]{:S(2)}) collective-permute-start(f32[8,16,16,8]{2,3,1,0:T(8,128)S(1)} %copy.96), channel_id=1, source_target_pairs={{0,1},{1,2},{2,3},{3,4},{4,5},{5,6},{6,7},{7,0},{8,9},{9,10},{10,1... | collective-permute-start | bytes 196616 | tf_op jit(solution)/shard_map/ppermute | solution.py:22
  106.4 5.3 %collective-permute-done.5 = f32[8,16,16,8]{2,3,1,0:T(8,128)S(1)} collective-permute-done((f32[8,16,16,8]{2,3,1,0:T(8,128)}, f32[8,16,16,8]{2,3,1,0:T(8,128)S(1)}, u32[]{:S(2)}, u32[]{:S(2)}) %collective-permute-start.5) | collective-permute-done | bytes 65568 | tf_op jit(solution)/shard_map/ppermute | solution.py:23
  112.1 13.2 %collective-permute-done.4 = f32[8,16,16,8]{2,3,1,0:T(8,128)} collective-permute-done((f32[8,16,16,8]{2,3,1,0:T(8,128)S(1)}, f32[8,16,16,8]{2,3,1,0:T(8,128)}, u32[]{:S(2)}, u32[]{:S(2)}) %collective-permute-start.4) | collective-permute-done | bytes 65568 | tf_op jit(solution)/shard_map/ppermute | solution.py:22
  125.2 1.4 copy.97
  126.6 8.6 %fusion.52 = f32[8,16,16,24]{3,2,1,0:T(8,128)S(1)} fusion(f32[8,16,16,8]{3,2,1,0:T(8,128)S(1)} %copy.99, f32[8,16,16,24]{3,2,1,0:T(8,128)S(1)} %fusion.10, f32[8,16,16,8]{3,2,1,0:T(8,128)S(1)} %copy.97, f32[8]{0:T(128)S(1)} %copy-done.1, f32[8]{0:T(128)S(1)} %copy-done.2, f32[8]{0:T(128)S(1)} %copy-done.3, f32[8]{0:T(128)S(1)} %copy-done.4, ...), kind=kLoop, calls=%fused_computation.87 | loop fusion | flops 2359296 | bytes 524544 | tf_op jit(solution)/shard_map/add | solution.py:47
  135.4 7.7 %fusion.6 = bf16[384,384]{0,1:T(8,128)(2,1)S(1)} fusion(bf16[16,16,24,384]{3,2,1,0:T(8,128)(2,1)} %param.55, f32[16,16,24]{2,1,0:T(8,128)S(1)} %fusion.92), kind=kOutput, calls=%fused_computation.40 | convolution fusion | flops 1821523968 | bytes 5038080 | tf_op jit(solution)/shard_map/dot_general | solution.py:135
  144.2 41.4 %all_to_all.16 = bf16[64,2,3072]{2,1,0:T(2,128)(2,1)S(1)} all-to-all(bf16[64,2,3072]{2,1,0:T(2,128)(2,1)S(1)} %reshape.278), channel_id=1, replica_groups=mesh['gx'=8,'gy'=8,'gz'=8] {'gx','gy'}, dimensions={0} | all-to-all | bytes 1572864 | tf_op jit(solution)/shard_map/all_to_all | solution.py:140
  186.2 0.8 copy.103
  (46 shorter events, 4.9 us)
Async XLA Ops:
  3.8 29.2 %all-to-all-start = ((s32[64,1,2]{2,1,0:T(1,128)}), s32[64,1,2]{2,1,0:T(1,128)S(1)}, u32[]{:S(2)}, u32[]{:S(2)}) async-start(s32[64,1,2]{2,1,0:T(1,128)} %bitcast), calls=%async_computation | async-start | bytes 65536 | tf_op jit(solution)/shard_map/all_to_all | solution.py:105
  32.9 31.0 %all-to-all-start.1 = ((bf16[64,2,3072]{2,1,0:T(2,128)(2,1)}), bf16[64,2,3072]{2,1,0:T(2,128)(2,1)S(1)}, u32[]{:S(2)}, u32[]{:S(2)}) async-start(bf16[64,2,3072]{2,1,0:T(2,128)(2,1)} %reshape.272), calls=%async_computation.1 | async-start | bytes 1572864 | tf_op jit(solution)/shard_map/all_to_all | solution.py:98
  71.2 9.2 %copy-start.1 = (f32[8]{0:T(128)S(1)}, f32[8]{0:T(128)}, u32[]{:S(2)}) copy-start(f32[8]{0:T(128)} %constant.68.clone) | copy-start | bytes 100
  71.2 9.2 %copy-start.2 = (f32[8]{0:T(128)S(1)}, f32[8]{0:T(128)}, u32[]{:S(2)}) copy-start(f32[8]{0:T(128)} %constant.67.clone) | copy-start | bytes 100
  71.2 9.1 %copy-start.3 = (f32[8]{0:T(128)S(1)}, f32[8]{0:T(128)}, u32[]{:S(2)}) copy-start(f32[8]{0:T(128)} %constant.66.clone) | copy-start | bytes 100
  71.2 9.1 %copy-start.4 = (f32[8]{0:T(128)S(1)}, f32[8]{0:T(128)}, u32[]{:S(2)}) copy-start(f32[8]{0:T(128)} %constant.65.clone) | copy-start | bytes 100
  71.3 9.1 %copy-start.5 = (f32[8]{0:T(128)S(1)}, f32[8]{0:T(128)}, u32[]{:S(2)}) copy-start(f32[8]{0:T(128)} %constant.64.clone) | copy-start | bytes 100
  71.3 9.1 %copy-start.6 = (f32[8]{0:T(128)S(1)}, f32[8]{0:T(128)}, u32[]{:S(2)}) copy-start(f32[8]{0:T(128)} %constant.63.clone) | copy-start | bytes 100
  71.3 9.1 %copy-start.7 = (f32[8]{0:T(128)S(1)}, f32[8]{0:T(128)}, u32[]{:S(2)}) copy-start(f32[8]{0:T(128)} %constant.62.clone) | copy-start | bytes 100
  71.3 9.1 %copy-start.8 = (f32[8]{0:T(128)S(1)}, f32[8]{0:T(128)}, u32[]{:S(2)}) copy-start(f32[8]{0:T(128)} %constant.61.clone) | copy-start | bytes 100
  71.5 7.5 %collective-permute-start.1 = (f32[8,16,24]{2,1,0:T(8,128)S(1)}, f32[8,16,24]{2,1,0:T(8,128)S(1)}, u32[]{:S(2)}, u32[]{:S(2)}) collective-permute-start(f32[8,16,24]{2,1,0:T(8,128)S(1)} %slice.246), channel_id=1, source_target_pairs={{64,0},{128,64},{192,128},{256,192},{320,256},{384,320},{448,384},... | collective-permute-start | bytes 36872 | tf_op jit(solution)/shard_map/ppermute | solution.py:23
  74.3 5.9 %collective-permute-start = (f32[8,16,24]{2,1,0:T(8,128)S(1)}, f32[8,16,24]{2,1,0:T(8,128)S(1)}, u32[]{:S(2)}, u32[]{:S(2)}) collective-permute-start(f32[8,16,24]{2,1,0:T(8,128)S(1)} %slice.244), channel_id=1, source_target_pairs={{0,64},{64,128},{128,192},{192,256},{256,320},{320,384},{384,448},... | collective-permute-start | bytes 36872 | tf_op jit(solution)/shard_map/ppermute | solution.py:22
  81.9 13.3 %collective-permute-start.2 = (f32[8,16,8,24]{3,2,1,0:T(8,128)S(1)}, f32[8,16,8,24]{3,2,1,0:T(8,128)S(1)}, u32[]{:S(2)}, u32[]{:S(2)}) collective-permute-start(f32[8,16,8,24]{3,2,1,0:T(8,128)S(1)} %get-tuple-element.10), channel_id=1, source_target_pairs={{0,8},{8,16},{16,24},{24,32},{32,40},{40,48},{48,56},{56,0},{1,9},... | collective-permute-start | bytes 294920 | tf_op jit(solution)/shard_map/ppermute | solution.py:22
  83.8 12.2 %collective-permute-start.3 = (f32[8,16,8,24]{3,2,1,0:T(8,128)S(1)}, f32[8,16,8,24]{3,2,1,0:T(8,128)S(1)}, u32[]{:S(2)}, u32[]{:S(2)}) collective-permute-start(f32[8,16,8,24]{3,2,1,0:T(8,128)S(1)} %get-tuple-element.11), channel_id=1, source_target_pairs={{8,0},{16,8},{24,16},{32,24},{40,32},{48,40},{56,48},{0,56},{9,1},... | collective-permute-start | bytes 294920 | tf_op jit(solution)/shard_map/ppermute | solution.py:23
  100.6 11.1 %collective-permute-start.5 = (f32[8,16,16,8]{2,3,1,0:T(8,128)}, f32[8,16,16,8]{2,3,1,0:T(8,128)S(1)}, u32[]{:S(2)}, u32[]{:S(2)}) collective-permute-start(f32[8,16,16,8]{2,3,1,0:T(8,128)} %copy.98), channel_id=1, source_target_pairs={{1,0},{2,1},{3,2},{4,3},{5,4},{6,5},{7,6},{0,7},{9,8},{10,9},{11,1... | collective-permute-start | bytes 196616 | tf_op jit(solution)/shard_map/ppermute | solution.py:23
  102.9 22.3 %collective-permute-start.4 = (f32[8,16,16,8]{2,3,1,0:T(8,128)S(1)}, f32[8,16,16,8]{2,3,1,0:T(8,128)}, u32[]{:S(2)}, u32[]{:S(2)}) collective-permute-start(f32[8,16,16,8]{2,3,1,0:T(8,128)S(1)} %copy.96), channel_id=1, source_target_pairs={{0,1},{1,2},{2,3},{3,4},{4,5},{5,6},{6,7},{7,0},{8,9},{9,10},{10,1... | collective-permute-start | bytes 196616 | tf_op jit(solution)/shard_map/ppermute | solution.py:22
  135.3 7.8 %copy-start = (f32[16,16,24]{2,1,0:T(8,128)}, f32[16,16,24]{2,1,0:T(8,128)S(1)}, u32[]{:S(2)}) copy-start(f32[16,16,24]{2,1,0:T(8,128)S(1)} %fusion.92) | copy-start | bytes 73732
where the time goes:
time: 188 us; the launch traced here: 187 us
  waiting for transfers between devices  54.9 us (29%)
  starting transfers between devices  41.9 us (22%)
  blocking collectives  41.4 us (22%)
  local copies, waits for them, and re-layouts  16.2 us (9%)
  other arithmetic  15.8 us (8%)
  matrix products  15.7 us (8%)
    all_to_all x1, blocking collectives, local(): lax.all_to_all(returned.reshape(tile_count, capacity, row_width), ('gx',...  41.4 us
    ppermute x3, waiting for transfers between devices, with_halo(): before = lax.ppermute(last, axis, up)  21.1 us
    all_to_all x1, waiting for transfers between devices, local(): lax.all_to_all(direct_out.reshape(tile_count, capacity, row_width), ('gx'...  18.8 us
    all_to_all x1, starting transfers between devices, local(): lax.all_to_all(direct_keys.reshape(tile_count, capacity), ('gx', 'gy'), s...  17.6 us
    add x3, other arithmetic, smooth_along(): running = addend if running is None else running + addend  13 us
    ppermute x3, starting transfers between devices, with_halo(): before = lax.ppermute(last, axis, up)  10 us
    ppermute x3, starting transfers between devices, with_halo(): after = lax.ppermute(initial, axis, down)  9.26 us
    all_to_all x1, waiting for transfers between devices, local(): lax.all_to_all(direct_keys.reshape(tile_count, capacity), ('gx', 'gy'), s...  8.79 us
  transfers between devices with their start and end apart: 8, of which 7 were waited for; matrix products, arithmetic and copies ran while one was open for 6% of the time, Pallas kernels for 0%

commit v1 on v0

v1 whole, which is shorter than its diff:
```python
import functools
import math

import jax
import jax.numpy as jnp
import numpy as np
from jax import lax
from jax.experimental import pallas as pl
from jax.experimental.pallas import tpu as pltpu
from jax.sharding import PartitionSpec as P

MESH = pl.DeviceIdType.MESH
RADIUS = 8
ALPHAS = (0.012, 0.025, 0.05, 0.1, 0.2, 0.4, 0.8, 1.6)
MIXES = (0.30, 0.30, 0.32, 0.34, 0.36, 0.38, 0.40, 0.42)
TERMS = len(ALPHAS)
F32 = jnp.float32
BF16 = jnp.bfloat16
I32 = jnp.int32


def filter_tables(tx):
    taps = np.array([[math.exp(-a * s * s) for s in range(RADIUS + 1)] for a in ALPHAS])
    norm = taps[:, 0] ** 2 + 2 * (taps[:, 1:] ** 2).sum(axis=1)
    mix = np.array(MIXES) / norm**1.5
    along_x = np.zeros((tx + 2 * RADIUS, TERMS, tx))
    for x in range(tx):
        for s in range(-RADIUS, RADIUS + 1):
            along_x[x + RADIUS + s, :, x] = taps[:, abs(s)]
    along_x = along_x.reshape(tx + 2 * RADIUS, TERMS * tx).astype(np.float32)
    lanes = np.zeros((32, TERMS * tx), np.float32)
    lanes[: RADIUS + 1] = np.repeat(taps, tx, axis=0).T
    lanes[16 : 16 + RADIUS + 1] = np.repeat(taps * mix[:, None], tx, axis=0).T
    return along_x, lanes


def iota(shape, dim):
    return lax.broadcasted_iota(I32, shape, dim)


def one_hot(mask):
    return jnp.where(mask, 1.0, 0.0).astype(BF16)


def split(a):
    high = a.astype(BF16)
    return high, (a - high.astype(F32)).astype(BF16)


def dot(a, b, ca=1, cb=0):
    return lax.dot_general(a, b, (((ca,), (cb,)), ((), ())), preferred_element_type=F32)


def kernel(
    dims,
    v_hbm, dm_hbm, tile_ref, place_ref, xmat_ref, taps_ref,
    pot_ref, own_ref,
    v, dm, vp, vtp, perm, hot_out, hot_out_t, hot_in, hot_in_t,
    key_out, key_in, out_buf, in_buf, ret_buf, back_buf,
    tmat, acc, halo, fx, fz, pot,
    local_sem, key_send, key_recv, pay_send, pay_recv,
    ret_send, ret_recv, halo_send, halo_recv,
):
    (nx, ny, nz), (tx, ty, tz), count, orb = dims
    tiles = nx * ny
    points = ty * tz
    gx, gy, gz = lax.axis_index("gx"), lax.axis_index("gy"), lax.axis_index("gz")
    me = gx * ny + gy

    def peer(step):
        px = lax.rem(gx + step // ny, nx)
        py = lax.rem(gy + lax.rem(step, ny), ny)
        return px, py, px * ny + py

    def near(d):
        return tuple(
            lax.rem(at + by + size, size) for at, by, size in zip((gx, gy, gz), d, (nx, ny, nz))
        )

    neighbours = [
        (dx, dy, dz)
        for dz in (0, 1, -1)
        for dy in (0, 1, -1)
        for dx in (0, 1, -1)
        if (dx, dy, dz) != (0, 0, 0)
    ]
    others = [d for d in neighbours if d[2] != 0]

    load_dm = pltpu.make_async_copy(dm_hbm, dm, local_sem.at[0])
    load_dm.start()
    load_v = pltpu.make_async_copy(v_hbm, v, local_sem.at[1])
    load_v.start()
    barrier = pltpu.get_barrier_semaphore()

    def greet(step, carry):
        px, py, _ = peer(step)
        pl.semaphore_signal(barrier, inc=1, device_id=(px, py, gz), device_id_type=MESH)
        return carry

    lax.fori_loop(1, tiles, greet, 0)
    for d in others:
        pl.semaphore_signal(barrier, inc=1, device_id=near(d), device_id_type=MESH)

    owners = tile_ref[...]
    places = place_ref[...].astype(F32) + 1.0
    mine = one_hot(iota((tiles, count), 0) == owners)
    before = one_hot(iota((count, count), 0) < iota((count, count), 1))
    rank = jnp.sum(dot(mine, before) * mine.astype(F32), axis=0, keepdims=True)
    slot = 2.0 * owners.astype(F32) + rank
    spread = one_hot(iota((count, orb), 1) // 8 == iota((count, orb), 0))
    wide = dot(jnp.broadcast_to(slot, (8, count)).astype(BF16), spread)[0:1]
    slot_row = (wide * 8.0).astype(I32) + (iota((1, orb), 1) & 7)
    for s in range(2):
        chosen = iota((tiles, count), 0) * 2 + s == slot.astype(I32)
        listed = jnp.where(chosen, places, 0.0).astype(BF16)
        key_out[:, s, :] = dot(listed, jnp.ones((count, 128), BF16))
    load_dm.wait()
    rows = 256

    def pack(i, carry):
        at = pl.ds(pl.multiple_of(i * rows, rows), rows)
        hot = one_hot(iota((rows, orb), 0) + i * rows == slot_row)
        hot_out[at, :] = hot
        out_buf[at, :] = dot(hot, dm[...]).astype(BF16)
        return carry

    lax.fori_loop(0, tiles * 16 // rows, pack, 0)

    pl.semaphore_wait(barrier, tiles - 1 + len(others))

    def block(ref, at):
        return ref.at[pl.ds(pl.multiple_of(at * 16, 16), 16), :]

    def send_keys(step, carry):
        px, py, at = peer(step)
        pltpu.make_async_remote_copy(
            src_ref=key_out.at[at], dst_ref=key_in.at[me], send_sem=key_send, recv_sem=key_recv,
            device_id=(px, py, gz), device_id_type=MESH,
        ).start()
        return carry

    def sender(src, dst, send_sem, recv_sem):
        def send(step, carry):
            px, py, at = peer(step)
            pltpu.make_async_remote_copy(
                src_ref=block(src, at), dst_ref=block(dst, me), send_sem=send_sem,
                recv_sem=recv_sem, device_id=(px, py, gz), device_id_type=MESH,
            ).start()
            return carry

        return send

    lax.fori_loop(1, tiles, send_keys, 0)
    pltpu.make_async_copy(key_out.at[me], key_in.at[me], key_recv).start()
    lax.fori_loop(1, tiles, sender(out_buf, in_buf, pay_send, pay_recv), 0)
    pltpu.make_async_copy(block(out_buf, me), block(in_buf, me), pay_recv).start()

    row, col = iota((points, points), 0), iota((points, points), 1)
    perm[...] = one_hot((row % ty) * tz + row // ty == col)
    load_v.wait()

    def reorder(c, carry):
        ordered = dot(perm[...], v[c]).astype(BF16)
        vp[c] = ordered
        vtp[c] = ordered.T
        return carry

    lax.fori_loop(0, tx, reorder, 0)

    pltpu.make_async_copy(key_in, key_in, key_recv).wait()
    row, lane = iota((128, orb), 0), iota((128, orb), 1)
    wanted = jnp.where((row & 7) == (lane & 7), lane // 8 + 1, -1).astype(F32)

    def place(i, carry):
        keys = key_in[pl.ds(i * 8, 8)]
        keys = jnp.broadcast_to(keys[:, :, None, :], (8, 2, 8, 128)).reshape(128, 128)
        hot = one_hot(jnp.concatenate([keys] * (orb // 128), axis=1) == wanted)
        at = pl.ds(pl.multiple_of(i * 128, 128), 128)
        hot_in[at, :] = hot
        hot_in_t[:, at] = hot.T
        hot_out_t[:, at] = hot_out[at, :].T
        return carry

    lax.fori_loop(0, tiles // 8, place, 0)

    pltpu.make_async_copy(in_buf, in_buf, pay_recv).wait()
    tmat[...] = dot(hot_in_t[...], in_buf[...]).astype(BF16)

    inner = ty * RADIUS

    def density(c, carry):
        values = vtp[c]
        mixed = dot(tmat[...], values)
        total = jnp.sum(mixed * values.astype(F32), axis=0, keepdims=True)
        halo[1, pl.ds(RADIUS + c, 1), pl.ds(inner, points)] = total
        return carry

    lax.fori_loop(0, tx, density, 0)

    row_ends = {0: ((RADIUS, tx), RADIUS), 1: ((tx, RADIUS), 0), -1: ((RADIUS, RADIUS), RADIUS + tx)}
    lane_ends = {0: ((inner, points), inner), 1: ((points, inner), 0), -1: ((inner, inner), inner + points)}
    copies = []
    for k, d in enumerate(neighbours):
        (r0, rn), r1 = row_ends[d[0]]
        (l0, ln), l1 = lane_ends[d[2]]
        copies.append(
            pltpu.make_async_remote_copy(
                src_ref=halo.at[1, pl.ds(r0, rn), pl.ds(l0, ln)],
                dst_ref=halo.at[1 - d[1], pl.ds(r1, rn), pl.ds(l1, ln)],
                send_sem=halo_send.at[k], recv_sem=halo_recv.at[k],
                device_id=near(d), device_id_type=MESH,
            )
        )
        copies[-1].start()
    for copy in copies:
        copy.wait_recv()

    for k, (cut, at) in enumerate((((ty - RADIUS, ty), 0), ((0, ty), RADIUS), ((0, RADIUS), RADIUS + ty))):
        high, low = split(halo[k])
        stacked = jnp.concatenate([high, low, high], axis=0)
        done = dot(stacked, xmat_ref[...], 0, 0).reshape(tz + 2 * RADIUS, ty, 128)
        fx[:, at : at + cut[1] - cut[0], :] = done[:, cut[0] : cut[1], :]

    def tap(s):
        return taps_ref[s : s + 1, :]

    for k in range((ty + 2 * RADIUS) // 8):
        at = pl.ds(8 * k, 8)
        total = tap(0) * fx[pl.ds(RADIUS, tz), at, :]
        for s in range(1, RADIUS + 1):
            total += tap(s) * (fx[pl.ds(RADIUS - s, tz), at, :] + fx[pl.ds(RADIUS + s, tz), at, :])
        fz[:, at, :] = total
    total = tap(16) * fz[:, pl.ds(RADIUS, ty), :]
    for s in range(1, RADIUS + 1):
        total += tap(16 + s) * (fz[:, pl.ds(RADIUS - s, ty), :] + fz[:, pl.ds(RADIUS + s, ty), :])
    both = jnp.concatenate(split(total.reshape(points, 128)), axis=1)
    gather = one_hot((iota((tx, 256), 1) & (tx - 1)) == iota((tx, 256), 0))
    pot[...] = dot(gather, both, 1, 1)

    weight = float(tx * points) ** (-0.5)
    acc[...] = jnp.zeros_like(acc)

    def gram(c, carry):
        scaled = pot[pl.ds(c, 1), :] * weight
        weighted = (vtp[c].astype(F32) * scaled).astype(BF16)
        acc[...] += dot(weighted, vp[c])
        return carry

    lax.fori_loop(0, tx, gram, 0)
    tmat[...] = acc[...].astype(BF16)

    def repack(i, carry):
        at = pl.ds(pl.multiple_of(i * rows, rows), rows)
        ret_buf[at, :] = dot(hot_in[at, :], tmat[...], 1, 1).astype(BF16)
        return carry

    lax.fori_loop(0, tiles * 16 // rows, repack, 0)
    lax.fori_loop(1, tiles, sender(ret_buf, back_buf, ret_send, ret_recv), 0)
    pltpu.make_async_copy(block(ret_buf, me), block(back_buf, me), ret_recv).start()

    high, rest = split(pot[...])
    rest = pot[...] - high.astype(F32)
    mid, low = split(rest)
    natural = dot(high, perm[...]) + (dot(mid, perm[...]) + dot(low, perm[...]))
    for y in range(ty):
        pot_ref[:, y, :] = natural[:, y * tz : (y + 1) * tz]

    for copy in copies:
        copy.wait_send()
    sent = key_out.at[pl.ds(0, tiles - 1)]
    pltpu.make_async_copy(sent, sent, key_send).wait()
    sent = out_buf.at[pl.ds(0, (tiles - 1) * 16), :]
    pltpu.make_async_copy(sent, sent, pay_send).wait()
    pltpu.make_async_copy(back_buf, back_buf, ret_recv).wait()
    own_ref[...] = dot(hot_out_t[...], back_buf[...]).astype(BF16)
    sent = ret_buf.at[pl.ds(0, (tiles - 1) * 16), :]
    pltpu.make_async_copy(sent, sent, ret_send).wait()


def solution(mesh):
    sizes = tuple(mesh.shape[a] for a in ("gx", "gy", "gz"))

    def local(values, slabs, slab_tile, slab_place):
        tx, ty, tz, orb = values.shape
        count = slabs.shape[0]
        points, tiles = ty * tz, sizes[0] * sizes[1]
        along_x, lanes = filter_tables(tx)
        high = along_x.astype(jnp.bfloat16)
        low = (along_x - high.astype(np.float32)).astype(jnp.bfloat16)
        xmat = np.concatenate([high, high, low], axis=0)
        wide = points + 2 * RADIUS * ty
        vm, any_ = pl.BlockSpec(memory_space=pltpu.VMEM), pl.BlockSpec(memory_space=pl.ANY)
        dma, slots = pltpu.SemaphoreType.DMA, tiles * 16
        pot, own = pl.pallas_call(
            functools.partial(kernel, (sizes, (tx, ty, tz), count, orb)),
            out_shape=(
                jax.ShapeDtypeStruct((tx, ty, tz), F32),
                jax.ShapeDtypeStruct((count * 8, orb), BF16),
            ),
            in_specs=[any_, any_, vm, vm, vm, vm],
            out_specs=(vm, vm),
            scratch_shapes=[
                pltpu.VMEM((tx, points, orb), BF16),
                pltpu.VMEM((count * 8, orb), BF16),
                pltpu.VMEM((tx, points, orb), BF16),
                pltpu.VMEM((tx, orb, points), BF16),
                pltpu.VMEM((points, points), BF16),
                pltpu.VMEM((slots, orb), BF16),
                pltpu.VMEM((orb, slots), BF16),
                pltpu.VMEM((slots, orb), BF16),
                pltpu.VMEM((orb, slots), BF16),
                pltpu.VMEM((tiles, 2, 128), F32),
                pltpu.VMEM((tiles, 2, 128), F32),
                pltpu.VMEM((slots, orb), BF16),
                pltpu.VMEM((slots, orb), BF16),
                pltpu.VMEM((slots, orb), BF16),
                pltpu.VMEM((slots, orb), BF16),
                pltpu.VMEM((orb, orb), BF16),
                pltpu.VMEM((orb, orb), F32),
                pltpu.VMEM((3, tx + 2 * RADIUS, wide), F32),
                pltpu.VMEM((tz + 2 * RADIUS, ty + 2 * RADIUS, 128), F32),
                pltpu.VMEM((tz, ty + 2 * RADIUS, 128), F32),
                pltpu.VMEM((tx, points), F32),
                dma((2,)), dma, dma, dma, dma, dma, dma, dma((26,)), dma((26,)),
            ],
            compiler_params=pltpu.CompilerParams(
                collective_id=0, has_side_effects=True, vmem_limit_bytes=56 * 1024 * 1024
            ),
        )(
            values.reshape(tx, points, orb),
            slabs.reshape(count * 8, orb),
            slab_tile.reshape(1, count),
            slab_place.reshape(1, count),
            jnp.asarray(xmat),
            jnp.asarray(lanes),
        )
        return pot, own.reshape(count, 8, orb)

    return jax.shard_map(
        local,
        mesh=mesh,
        in_specs=(
            P("gx", "gy", "gz", None),
            P(("gx", "gy", "gz"), None, None),
            P(("gx", "gy", "gz")),
            P(("gx", "gy", "gz")),
        ),
        out_specs=(P("gx", "gy", "gz"), P(("gx", "gy", "gz"), None, None)),
        check_vma=False,
    )
```

time: 188 us -> 90.6 us (0.48)
  the two profiles are of different devices: /device:TPU:1 before, /device:TPU:15 now
where the time goes in v1:
time: 90.6 us; the launch traced here: 90.4 us
  Pallas kernels  86.5 us (95%)
  local copies, waits for them, and re-layouts  3.27 us (4%)
    pallas_call x1, Pallas kernels, local(): pl.pallas_call(functools.partial(kernel, (sizes, (tx, ty, tz), count, orb...  86.5 us
    unnamed x2, local copies, waits for them, and re-layouts  3.27 us

profile of v1, /device:TPU:15, one launch (start us, length us, event | category | flops | bytes accessed | tf_op | source)
XLA Modules:
  0.0 90.4 jit_solution(2529044080448076426)
XLA Ops:
  0.6 86.5 %shard_map.77 = (f32[16,16,24]{2,1,0:T(8,128)}, bf16[384,384]{1,0:T(8,128)(2,1)}) custom-call(bf16[16,384,384]{2,1,0:T(8,128)(2,1)} %bitcast.5, bf16[384,384]{1,0:T(8,128)(2,1)} %bitcast.6, s32[1,48]{1,0:T(1,128)} %bitcast.8, s32[1,48]{1,0:T(1,128)} %bitcast.9, bf16[96,128]{1,0:T(8,128)(2,1)} %constant.4.clone.xmat_ref, f32[32,128]{1,0:T(8,128)} %constant.5.clone.taps_ref), custom_call_target="tpu_custom_call" | custom-call | tf_op jit(solution)/shard_map/pallas_call | solution.py:294
  87.1 1.6 %copy.10 = f32[16,16,24]{2,1,0:T(8,128)} copy(f32[16,16,24]{2,1,0:T(8,128)} %get-tuple-element.8) | data formatting | bytes 49152
  88.7 1.7 %copy.11 = bf16[48,8,384]{2,1,0:T(8,128)(2,1)} copy(bf16[48,8,384]{2,1,0:T(8,128)(2,1)} %bitcast.7) | data formatting | bytes 589824

commit v2 on v1

--- a/solution.py
+++ b/solution.py
@@ -68,8 +68,9 @@
     me = gx * ny + gy
 
     def peer(step):
-        px = lax.rem(gx + step // ny, nx)
-        py = lax.rem(gy + lax.rem(step, ny), ny)
+        back = tiles - step
+        px = lax.rem(gx + back // ny, nx)
+        py = lax.rem(gy + lax.rem(back, ny), ny)
         return px, py, px * ny + py
 
     def near(d):
@@ -79,9 +80,9 @@
 
     neighbours = [
         (dx, dy, dz)
-        for dz in (0, 1, -1)
-        for dy in (0, 1, -1)
-        for dx in (0, 1, -1)
+        for dz in (1, -1, 0)
+        for dx in (1, -1, 0)
+        for dy in (1, -1, 0)
         if (dx, dy, dz) != (0, 0, 0)
     ]
     others = [d for d in neighbours if d[2] != 0]
@@ -110,10 +111,13 @@
     spread = one_hot(iota((count, orb), 1) // 8 == iota((count, orb), 0))
     wide = dot(jnp.broadcast_to(slot, (8, count)).astype(BF16), spread)[0:1]
     slot_row = (wide * 8.0).astype(I32) + (iota((1, orb), 1) & 7)
-    for s in range(2):
-        chosen = iota((tiles, count), 0) * 2 + s == slot.astype(I32)
-        listed = jnp.where(chosen, places, 0.0).astype(BF16)
-        key_out[:, s, :] = dot(listed, jnp.ones((count, 128), BF16))
+    listed = [
+        jnp.where(iota((tiles, count), 0) * 2 + s == slot.astype(I32), places, 0.0).astype(BF16)
+        for s in range(2)
+    ]
+    key_out[:, 0, :] = sum(
+        dot(listed[s], one_hot(iota((count, 128), 1) == 64 * s)) for s in range(2)
+    )
     load_dm.wait()
     rows = 256
 
@@ -124,7 +128,7 @@
         out_buf[at, :] = dot(hot, dm[...]).astype(BF16)
         return carry
 
-    lax.fori_loop(0, tiles * 16 // rows, pack, 0)
+    lax.fori_loop(0, tiles * 16 // rows, pack, 0, unroll=True)
 
     pl.semaphore_wait(barrier, tiles - 1 + len(others))
 
@@ -165,15 +169,17 @@
         vtp[c] = ordered.T
         return carry
 
-    lax.fori_loop(0, tx, reorder, 0)
+    lax.fori_loop(0, tx, reorder, 0, unroll=4)
 
     pltpu.make_async_copy(key_in, key_in, key_recv).wait()
     row, lane = iota((128, orb), 0), iota((128, orb), 1)
+    ours = (iota((128, 128), 1) // 64) == ((iota((128, 128), 0) // 8) & 1)
     wanted = jnp.where((row & 7) == (lane & 7), lane // 8 + 1, -1).astype(F32)
 
     def place(i, carry):
         keys = key_in[pl.ds(i * 8, 8)]
-        keys = jnp.broadcast_to(keys[:, :, None, :], (8, 2, 8, 128)).reshape(128, 128)
+        keys = jnp.broadcast_to(keys, (8, 16, 128)).reshape(128, 128)
+        keys = dot(jnp.where(ours, keys, 0.0).astype(BF16), jnp.ones((128, 128), BF16))
         hot = one_hot(jnp.concatenate([keys] * (orb // 128), axis=1) == wanted)
         at = pl.ds(pl.multiple_of(i * 128, 128), 128)
         hot_in[at, :] = hot
@@ -181,7 +187,7 @@
         hot_out_t[:, at] = hot_out[at, :].T
         return carry
 
-    lax.fori_loop(0, tiles // 8, place, 0)
+    lax.fori_loop(0, tiles // 8, place, 0, unroll=2)
 
     pltpu.make_async_copy(in_buf, in_buf, pay_recv).wait()
     tmat[...] = dot(hot_in_t[...], in_buf[...]).astype(BF16)
@@ -195,7 +201,7 @@
         halo[1, pl.ds(RADIUS + c, 1), pl.ds(inner, points)] = total
         return carry
 
-    lax.fori_loop(0, tx, density, 0)
+    lax.fori_loop(0, tx, density, 0, unroll=True)
 
     row_ends = {0: ((RADIUS, tx), RADIUS), 1: ((tx, RADIUS), 0), -1: ((RADIUS, RADIUS), RADIUS + tx)}
     lane_ends = {0: ((inner, points), inner), 1: ((points, inner), 0), -1: ((inner, inner), inner + points)}
@@ -240,13 +246,11 @@
     weight = float(tx * points) ** (-0.5)
     acc[...] = jnp.zeros_like(acc)
 
-    def gram(c, carry):
-        scaled = pot[pl.ds(c, 1), :] * weight
-        weighted = (vtp[c].astype(F32) * scaled).astype(BF16)
-        acc[...] += dot(weighted, vp[c])
-        return carry
-
-    lax.fori_loop(0, tx, gram, 0)
+    for c in range(0, tx, 4):
+        weighted = [
+            (vtp[k].astype(F32) * (pot[k : k + 1, :] * weight)).astype(BF16) for k in range(c, c + 4)
+        ]
+        acc[...] += dot(jnp.concatenate(weighted, axis=1), vp[c : c + 4].reshape(4 * points, orb))
     tmat[...] = acc[...].astype(BF16)
 
     def repack(i, carry):
@@ -254,7 +258,7 @@
         ret_buf[at, :] = dot(hot_in[at, :], tmat[...], 1, 1).astype(BF16)
         return carry
 
-    lax.fori_loop(0, tiles * 16 // rows, repack, 0)
+    lax.fori_loop(0, tiles * 16 // rows, repack, 0, unroll=True)
     lax.fori_loop(1, tiles, sender(ret_buf, back_buf, ret_send, ret_recv), 0)
     pltpu.make_async_copy(block(ret_buf, me), block(back_buf, me), ret_recv).start()
 
@@ -275,6 +279,17 @@
     own_ref[...] = dot(hot_out_t[...], back_buf[...]).astype(BF16)
     sent = ret_buf.at[pl.ds(0, (tiles - 1) * 16), :]
     pltpu.make_async_copy(sent, sent, ret_send).wait()
+
+
+def hand_over(pot_ref, own_ref, pot_out, own_out, sem):
+    copies = [
+        pltpu.make_async_copy(pot_ref, pot_out, sem.at[0]),
+        pltpu.make_async_copy(own_ref, own_out, sem.at[1]),
+    ]
+    for copy in copies:
+        copy.start()
+    for copy in copies:
+        copy.wait()
 
 
 def solution(mesh):
@@ -309,8 +324,8 @@
                 pltpu.VMEM((orb, slots), BF16),
                 pltpu.VMEM((slots, orb), BF16),
                 pltpu.VMEM((orb, slots), BF16),
-                pltpu.VMEM((tiles, 2, 128), F32),
-                pltpu.VMEM((tiles, 2, 128), F32),
+                pltpu.VMEM((tiles, 1, 128), F32),
+                pltpu.VMEM((tiles, 1, 128), F32),
                 pltpu.VMEM((slots, orb), BF16),
                 pltpu.VMEM((slots, orb), BF16),
                 pltpu.VMEM((slots, orb), BF16),
@@ -334,6 +349,16 @@
             jnp.asarray(xmat),
             jnp.asarray(lanes),
         )
+        pot, own = pl.pallas_call(
+            hand_over,
+            out_shape=(
+                jax.ShapeDtypeStruct((tx, ty, tz), F32),
+                jax.ShapeDtypeStruct((count * 8, orb), BF16),
+            ),
+            in_specs=[any_, any_],
+            out_specs=(any_, any_),
+            scratch_shapes=[dma((2,))],
+        )(pot, own)
         return pot, own.reshape(count, 8, orb)
 
     return jax.shard_map(

time: 90.6 us -> 96.5 us (1.065)
  the two profiles are of different devices: /device:TPU:15 before, /device:TPU:62 now
where the time goes in v2:
time: 96.5 us; the launch traced here: 96.3 us
  Pallas kernels  95.7 us (99%)
    pallas_call x1, Pallas kernels, local(): pl.pallas_call(functools.partial(kernel, (sizes, (tx, ty, tz), count, orb...  81.7 us
    pallas_call x1, Pallas kernels, local(): pl.pallas_call(hand_over, out_shape=(jax.ShapeDtypeStruct((tx, ty, tz), F...  14 us

profile of v2, /device:TPU:62, one launch (start us, length us, event | category | flops | bytes accessed | tf_op | source)
XLA Modules:
  0.0 96.3 jit_solution(7502800600651321305)
XLA Ops:
  0.6 81.7 %shard_map.77 = (f32[16,16,24]{2,1,0:T(8,128)}, bf16[384,384]{1,0:T(8,128)(2,1)}) custom-call(bf16[16,384,384]{2,1,0:T(8,128)(2,1)} %bitcast.5, bf16[384,384]{1,0:T(8,128)(2,1)} %bitcast.6, s32[1,48]{1,0:T(1,128)} %bitcast.7, s32[1,48]{1,0:T(1,128)} %bitcast.8, bf16[96,128]{1,0:T(8,128)(2,1)} %constant.4.clone.xmat_ref, f32[32,128]{1,0:T(8,128)} %constant.5.clone.taps_ref), custom_call_target="tpu_custom_call" | custom-call | tf_op jit(solution)/shard_map/pallas_call | solution.py:309
  82.3 14.0 %shard_map.78 = (f32[16,16,24]{2,1,0:T(8,128)}, bf16[384,384]{1,0:T(8,128)(2,1)}) custom-call(f32[16,16,24]{2,1,0:T(8,128)} %get-tuple-element.6.pot_ref, bf16[384,384]{1,0:T(8,128)(2,1)} %get-tuple-element.7.own_ref), custom_call_target="tpu_custom_call" | custom-call | tf_op jit(solution)/shard_map/pallas_call | solution.py:352

commit v3 on v2

--- a/solution.py
+++ b/solution.py
@@ -53,12 +53,12 @@
 
 def kernel(
     dims,
-    v_hbm, dm_hbm, tile_ref, place_ref, xmat_ref, taps_ref,
+    v_hbm, dm_hbm, tile_hbm, place_hbm, xmat_hbm, taps_hbm,
     pot_ref, own_ref,
     v, dm, vp, vtp, perm, hot_out, hot_out_t, hot_in, hot_in_t,
     key_out, key_in, out_buf, in_buf, ret_buf, back_buf,
     tmat, acc, halo, fx, fz, pot,
-    local_sem, key_send, key_recv, pay_send, pay_recv,
+    tile_ref, place_ref, xmat_ref, taps_ref, local_sem, key_send, key_recv, pay_send, pay_recv,
     ret_send, ret_recv, halo_send, halo_recv,
 ):
     (nx, ny, nz), (tx, ty, tz), count, orb = dims
@@ -87,10 +87,15 @@
     ]
     others = [d for d in neighbours if d[2] != 0]
 
-    load_dm = pltpu.make_async_copy(dm_hbm, dm, local_sem.at[0])
-    load_dm.start()
-    load_v = pltpu.make_async_copy(v_hbm, v, local_sem.at[1])
-    load_v.start()
+    loads = [
+        pltpu.make_async_copy(*pair, local_sem.at[k])
+        for k, pair in enumerate((
+            (tile_hbm, tile_ref), (place_hbm, place_ref), (dm_hbm, dm),
+            (v_hbm, v), (xmat_hbm, xmat_ref), (taps_hbm, taps_ref),
+        ))
+    ]
+    for load in loads:
+        load.start()
     barrier = pltpu.get_barrier_semaphore()
 
     def greet(step, carry):
@@ -102,6 +107,8 @@
     for d in others:
         pl.semaphore_signal(barrier, inc=1, device_id=near(d), device_id_type=MESH)
 
+    loads[0].wait()
+    loads[1].wait()
     owners = tile_ref[...]
     places = place_ref[...].astype(F32) + 1.0
     mine = one_hot(iota((tiles, count), 0) == owners)
@@ -118,7 +125,7 @@
     key_out[:, 0, :] = sum(
         dot(listed[s], one_hot(iota((count, 128), 1) == 64 * s)) for s in range(2)
     )
-    load_dm.wait()
+    loads[2].wait()
     rows = 256
 
     def pack(i, carry):
@@ -148,20 +155,36 @@
             px, py, at = peer(step)
             pltpu.make_async_remote_copy(
                 src_ref=block(src, at), dst_ref=block(dst, me), send_sem=send_sem,
-                recv_sem=recv_sem, device_id=(px, py, gz), device_id_type=MESH,
+                recv_sem=recv_sem.at[gx], device_id=(px, py, gz), device_id_type=MESH,
             ).start()
             return carry
 
         return send
+
+    span = ny * 16
+
+    def gathered(hot_t, buf, sem):
+        acc[...] = jnp.zeros_like(acc)
+
+        def add(step, carry):
+            at = lax.rem(gx + step, nx)
+            part = pl.ds(pl.multiple_of(at * span, span), span)
+            pltpu.make_async_copy(buf.at[part, :], buf.at[part, :], sem.at[at]).wait()
+            acc[...] += dot(hot_t[:, part], buf[part, :])
+            return carry
+
+        lax.fori_loop(1, nx + 1, add, 0)
+        return acc[...].astype(BF16)
 
     lax.fori_loop(1, tiles, send_keys, 0)
     pltpu.make_async_copy(key_out.at[me], key_in.at[me], key_recv).start()
     lax.fori_loop(1, tiles, sender(out_buf, in_buf, pay_send, pay_recv), 0)
-    pltpu.make_async_copy(block(out_buf, me), block(in_buf, me), pay_recv).start()
+    pltpu.make_async_copy(block(out_buf, me), block(in_buf, me), pay_recv.at[gx]).start()
 
     row, col = iota((points, points), 0), iota((points, points), 1)
     perm[...] = one_hot((row % ty) * tz + row // ty == col)
-    load_v.wait()
+    for load in loads[3:]:
+        load.wait()
 
     def reorder(c, carry):
         ordered = dot(perm[...], v[c]).astype(BF16)
@@ -189,8 +212,7 @@
 
     lax.fori_loop(0, tiles // 8, place, 0, unroll=2)
 
-    pltpu.make_async_copy(in_buf, in_buf, pay_recv).wait()
-    tmat[...] = dot(hot_in_t[...], in_buf[...]).astype(BF16)
+    tmat[...] = gathered(hot_in_t, in_buf, pay_recv)
 
     inner = ty * RADIUS
 
@@ -260,7 +282,7 @@
 
     lax.fori_loop(0, tiles * 16 // rows, repack, 0, unroll=True)
     lax.fori_loop(1, tiles, sender(ret_buf, back_buf, ret_send, ret_recv), 0)
-    pltpu.make_async_copy(block(ret_buf, me), block(back_buf, me), ret_recv).start()
+    pltpu.make_async_copy(block(ret_buf, me), block(back_buf, me), ret_recv.at[gx]).start()
 
     high, rest = split(pot[...])
     rest = pot[...] - high.astype(F32)
@@ -275,21 +297,14 @@
     pltpu.make_async_copy(sent, sent, key_send).wait()
     sent = out_buf.at[pl.ds(0, (tiles - 1) * 16), :]
     pltpu.make_async_copy(sent, sent, pay_send).wait()
-    pltpu.make_async_copy(back_buf, back_buf, ret_recv).wait()
-    own_ref[...] = dot(hot_out_t[...], back_buf[...]).astype(BF16)
+    own_ref[...] = gathered(hot_out_t, back_buf, ret_recv)
     sent = ret_buf.at[pl.ds(0, (tiles - 1) * 16), :]
     pltpu.make_async_copy(sent, sent, ret_send).wait()
 
 
-def hand_over(pot_ref, own_ref, pot_out, own_out, sem):
-    copies = [
-        pltpu.make_async_copy(pot_ref, pot_out, sem.at[0]),
-        pltpu.make_async_copy(own_ref, own_out, sem.at[1]),
-    ]
-    for copy in copies:
-        copy.start()
-    for copy in copies:
-        copy.wait()
+def hand_over(pot_ref, own_ref, pot_out, own_out):
+    pot_out[...] = pot_ref[...]
+    own_out[...] = own_ref[...]
 
 
 def solution(mesh):
@@ -312,7 +327,7 @@
                 jax.ShapeDtypeStruct((tx, ty, tz), F32),
                 jax.ShapeDtypeStruct((count * 8, orb), BF16),
             ),
-            in_specs=[any_, any_, vm, vm, vm, vm],
+            in_specs=[any_] * 6,
             out_specs=(vm, vm),
             scratch_shapes=[
                 pltpu.VMEM((tx, points, orb), BF16),
@@ -336,7 +351,11 @@
                 pltpu.VMEM((tz + 2 * RADIUS, ty + 2 * RADIUS, 128), F32),
                 pltpu.VMEM((tz, ty + 2 * RADIUS, 128), F32),
                 pltpu.VMEM((tx, points), F32),
-                dma((2,)), dma, dma, dma, dma, dma, dma, dma((26,)), dma((26,)),
+                pltpu.VMEM((1, count), I32),
+                pltpu.VMEM((1, count), I32),
+                pltpu.VMEM(xmat.shape, BF16),
+                pltpu.VMEM(lanes.shape, F32),
+                dma((6,)), dma, dma, dma, dma((sizes[0],)), dma, dma((sizes[0],)), dma((26,)), dma((26,)),
             ],
             compiler_params=pltpu.CompilerParams(
                 collective_id=0, has_side_effects=True, vmem_limit_bytes=56 * 1024 * 1024
@@ -355,9 +374,8 @@
                 jax.ShapeDtypeStruct((tx, ty, tz), F32),
                 jax.ShapeDtypeStruct((count * 8, orb), BF16),
             ),
-            in_specs=[any_, any_],
-            out_specs=(any_, any_),
-            scratch_shapes=[dma((2,))],
+            in_specs=[vm, vm],
+            out_specs=(vm, vm),
         )(pot, own)
         return pot, own.reshape(count, 8, orb)
 

time: 96.5 us -> 83.5 us (0.87)
  the two profiles are of different devices: /device:TPU:62 before, /device:TPU:80 now
where the time goes in v3:
time: 83.5 us; the launch traced here: 83.3 us
  Pallas kernels  82.7 us (99%)
    pallas_call x1, Pallas kernels, local(): pl.pallas_call(functools.partial(kernel, (sizes, (tx, ty, tz), count, orb...  80.9 us
    pallas_call x1, Pallas kernels, local(): pl.pallas_call(hand_over, out_shape=(jax.ShapeDtypeStruct((tx, ty, tz), F...  1.8 us

profile of v3, /device:TPU:80, one launch (start us, length us, event | category | flops | bytes accessed | tf_op | source)
XLA Modules:
  0.0 83.3 jit_solution(7041425756109412530)
XLA Ops:
  0.6 80.9 %shard_map.77 = (f32[16,16,24]{2,1,0:T(8,128)}, bf16[384,384]{1,0:T(8,128)(2,1)}) custom-call(bf16[16,384,384]{2,1,0:T(8,128)(2,1)} %bitcast.5, bf16[384,384]{1,0:T(8,128)(2,1)} %bitcast.6, s32[1,48]{1,0:T(1,128)} %bitcast.7, s32[1,48]{1,0:T(1,128)} %bitcast.8, bf16[96,128]{1,0:T(8,128)(2,1)} %constant.4.clone.xmat_hbm, f32[32,128]{1,0:T(8,128)} %constant.5.clone.taps_hbm), custom_call_target="tpu_custom_call" | custom-call | tf_op jit(solution)/shard_map/pallas_call | solution.py:324
  81.5 1.8 %shard_map.78 = (f32[16,16,24]{2,1,0:T(8,128)}, bf16[384,384]{1,0:T(8,128)(2,1)}) custom-call(f32[16,16,24]{2,1,0:T(8,128)} %get-tuple-element.6.pot_ref, bf16[384,384]{1,0:T(8,128)(2,1)} %get-tuple-element.7.own_ref), custom_call_target="tpu_custom_call" | custom-call | tf_op jit(solution)/shard_map/pallas_call | solution.py:371

commit v4 on v3

--- a/solution.py
+++ b/solution.py
@@ -139,8 +139,8 @@
 
     pl.semaphore_wait(barrier, tiles - 1 + len(others))
 
-    def block(ref, at):
-        return ref.at[pl.ds(pl.multiple_of(at * 16, 16), 16), :]
+    def block(ref, at, cols):
+        return ref.at[pl.ds(pl.multiple_of(at * 16, 16), 16), pl.ds(cols[0], cols[1] - cols[0])]
 
     def send_keys(step, carry):
         px, py, at = peer(step)
@@ -150,36 +150,39 @@
         ).start()
         return carry
 
-    def sender(src, dst, send_sem, recv_sem):
+    def exchange(src, dst, send_sem, recv_sem, cols):
         def send(step, carry):
             px, py, at = peer(step)
             pltpu.make_async_remote_copy(
-                src_ref=block(src, at), dst_ref=block(dst, me), send_sem=send_sem,
+                src_ref=block(src, at, cols), dst_ref=block(dst, me, cols), send_sem=send_sem,
                 recv_sem=recv_sem.at[gx], device_id=(px, py, gz), device_id_type=MESH,
             ).start()
             return carry
 
-        return send
+        lax.fori_loop(1, tiles, send, 0)
+        pltpu.make_async_copy(block(src, me, cols), block(dst, me, cols), recv_sem.at[gx]).start()
 
     span = ny * 16
 
-    def gathered(hot_t, buf, sem):
-        acc[...] = jnp.zeros_like(acc)
+    def gathered(hot_t, buf, sem, cols):
+        to = pl.ds(cols[0], cols[1] - cols[0])
+        acc[:, to] = jnp.zeros_like(acc[:, to])
 
         def add(step, carry):
             at = lax.rem(gx + step, nx)
             part = pl.ds(pl.multiple_of(at * span, span), span)
-            pltpu.make_async_copy(buf.at[part, :], buf.at[part, :], sem.at[at]).wait()
-            acc[...] += dot(hot_t[:, part], buf[part, :])
+            pltpu.make_async_copy(buf.at[part, to], buf.at[part, to], sem.at[at]).wait()
+            acc[:, to] += dot(hot_t[:, part], buf[part, to])
             return carry
 
         lax.fori_loop(1, nx + 1, add, 0)
-        return acc[...].astype(BF16)
+        return acc[:, to]
 
     lax.fori_loop(1, tiles, send_keys, 0)
     pltpu.make_async_copy(key_out.at[me], key_in.at[me], key_recv).start()
-    lax.fori_loop(1, tiles, sender(out_buf, in_buf, pay_send, pay_recv), 0)
-    pltpu.make_async_copy(block(out_buf, me), block(in_buf, me), pay_recv.at[gx]).start()
+    there, home = ((0, 256), (256, orb)), ((0, 128), (128, orb))
+    for k, cols in enumerate(there):
+        exchange(out_buf, in_buf, pay_send, pay_recv.at[k], cols)
 
     row, col = iota((points, points), 0), iota((points, points), 1)
     perm[...] = one_hot((row % ty) * tz + row // ty == col)
@@ -212,18 +215,19 @@
 
     lax.fori_loop(0, tiles // 8, place, 0, unroll=2)
 
-    tmat[...] = gathered(hot_in_t, in_buf, pay_recv)
-
     inner = ty * RADIUS
-
-    def density(c, carry):
-        values = vtp[c]
-        mixed = dot(tmat[...], values)
-        total = jnp.sum(mixed * values.astype(F32), axis=0, keepdims=True)
-        halo[1, pl.ds(RADIUS + c, 1), pl.ds(inner, points)] = total
-        return carry
-
-    lax.fori_loop(0, tx, density, 0, unroll=True)
+    for k, cols in enumerate(there):
+        part = pl.ds(cols[0], cols[1] - cols[0])
+        tmat[part, :] = gathered(hot_in_t, in_buf, pay_recv.at[k], cols).T.astype(BF16)
+
+        def density(c, carry, k=k, part=part):
+            mixed = dot(tmat[part, :], vtp[c])
+            total = jnp.sum(mixed * vtp[c, part, :].astype(F32), axis=0, keepdims=True)
+            at = halo.at[1, pl.ds(RADIUS + c, 1), pl.ds(inner, points)]
+            at[...] = total if k == 0 else at[...] + total
+            return carry
+
+        lax.fori_loop(0, tx, density, 0, unroll=True)
 
     row_ends = {0: ((RADIUS, tx), RADIUS), 1: ((tx, RADIUS), 0), -1: ((RADIUS, RADIUS), RADIUS + tx)}
     lane_ends = {0: ((inner, points), inner), 1: ((points, inner), 0), -1: ((inner, inner), inner + points)}
@@ -266,23 +270,25 @@
     pot[...] = dot(gather, both, 1, 1)
 
     weight = float(tx * points) ** (-0.5)
-    acc[...] = jnp.zeros_like(acc)
-
-    for c in range(0, tx, 4):
-        weighted = [
-            (vtp[k].astype(F32) * (pot[k : k + 1, :] * weight)).astype(BF16) for k in range(c, c + 4)
-        ]
-        acc[...] += dot(jnp.concatenate(weighted, axis=1), vp[c : c + 4].reshape(4 * points, orb))
-    tmat[...] = acc[...].astype(BF16)
-
-    def repack(i, carry):
-        at = pl.ds(pl.multiple_of(i * rows, rows), rows)
-        ret_buf[at, :] = dot(hot_in[at, :], tmat[...], 1, 1).astype(BF16)
-        return carry
-
-    lax.fori_loop(0, tiles * 16 // rows, repack, 0, unroll=True)
-    lax.fori_loop(1, tiles, sender(ret_buf, back_buf, ret_send, ret_recv), 0)
-    pltpu.make_async_copy(block(ret_buf, me), block(back_buf, me), ret_recv.at[gx]).start()
+    for k, cols in enumerate(home):
+        part = pl.ds(cols[0], cols[1] - cols[0])
+        acc[part, :] = jnp.zeros_like(acc[part, :])
+        for c in range(0, tx, 4):
+            weighted = [
+                (vtp[i, part, :].astype(F32) * (pot[i : i + 1, :] * weight)).astype(BF16)
+                for i in range(c, c + 4)
+            ]
+            whole = vp[c : c + 4].reshape(4 * points, orb)
+            acc[part, :] += dot(jnp.concatenate(weighted, axis=1), whole)
+        tmat[part, :] = acc[part, :].astype(BF16)
+
+        def repack(i, carry, part=part):
+            at = pl.ds(pl.multiple_of(i * rows, rows), rows)
+            ret_buf[at, part] = dot(hot_in[at, :], tmat[part, :], 1, 1).astype(BF16)
+            return carry
+
+        lax.fori_loop(0, tiles * 16 // rows, repack, 0, unroll=True)
+        exchange(ret_buf, back_buf, ret_send, ret_recv.at[k], cols)
 
     high, rest = split(pot[...])
     rest = pot[...] - high.astype(F32)
@@ -297,7 +303,8 @@
     pltpu.make_async_copy(sent, sent, key_send).wait()
     sent = out_buf.at[pl.ds(0, (tiles - 1) * 16), :]
     pltpu.make_async_copy(sent, sent, pay_send).wait()
-    own_ref[...] = gathered(hot_out_t, back_buf, ret_recv)
+    for k, cols in enumerate(home):
+        own_ref[:, cols[0] : cols[1]] = gathered(hot_out_t, back_buf, ret_recv.at[k], cols).astype(BF16)
     sent = ret_buf.at[pl.ds(0, (tiles - 1) * 16), :]
     pltpu.make_async_copy(sent, sent, ret_send).wait()
 
@@ -355,7 +362,8 @@
                 pltpu.VMEM((1, count), I32),
                 pltpu.VMEM(xmat.shape, BF16),
                 pltpu.VMEM(lanes.shape, F32),
-                dma((6,)), dma, dma, dma, dma((sizes[0],)), dma, dma((sizes[0],)), dma((26,)), dma((26,)),
+                dma((6,)), dma, dma, dma, dma((2, sizes[0])), dma, dma((2, sizes[0])),
+                dma((26,)), dma((26,)),
             ],
             compiler_params=pltpu.CompilerParams(
                 collective_id=0, has_side_effects=True, vmem_limit_bytes=56 * 1024 * 1024

time: 83.5 us -> 78.6 us (0.941)
  the two profiles are of different devices: /device:TPU:80 before, /device:TPU:1 now
where the time goes in v4:
time: 78.6 us; the launch traced here: 78.4 us
  Pallas kernels  77.8 us (99%)
    pallas_call x1, Pallas kernels, local(): pl.pallas_call(functools.partial(kernel, (sizes, (tx, ty, tz), count, orb...  76 us
    pallas_call x1, Pallas kernels, local(): pl.pallas_call(hand_over, out_shape=(jax.ShapeDtypeStruct((tx, ty, tz), F...  1.8 us

profile of v4, /device:TPU:1, one launch (start us, length us, event | category | flops | bytes accessed | tf_op | source)
XLA Modules:
  0.0 78.4 jit_solution(2228745165589904131)
XLA Ops:
  0.6 76.0 %shard_map.77 = (f32[16,16,24]{2,1,0:T(8,128)}, bf16[384,384]{1,0:T(8,128)(2,1)}) custom-call(bf16[16,384,384]{2,1,0:T(8,128)(2,1)} %bitcast.5, bf16[384,384]{1,0:T(8,128)(2,1)} %bitcast.6, s32[1,48]{1,0:T(1,128)} %bitcast.7, s32[1,48]{1,0:T(1,128)} %bitcast.8, bf16[96,128]{1,0:T(8,128)(2,1)} %constant.4.clone.xmat_hbm, f32[32,128]{1,0:T(8,128)} %constant.5.clone.taps_hbm), custom_call_target="tpu_custom_call" | custom-call | tf_op jit(solution)/shard_map/pallas_call | solution.py:331
  76.6 1.8 %shard_map.78 = (f32[16,16,24]{2,1,0:T(8,128)}, bf16[384,384]{1,0:T(8,128)(2,1)}) custom-call(f32[16,16,24]{2,1,0:T(8,128)} %get-tuple-element.6.pot_ref, bf16[384,384]{1,0:T(8,128)(2,1)} %get-tuple-element.7.own_ref), custom_call_target="tpu_custom_call" | custom-call | tf_op jit(solution)/shard_map/pallas_call | solution.py:379
